TPU v7x, 256 devices: a whole 4x4x8 slice. The times are simulated.
256 devices in a mesh: arc: 16 (over x, y_lo, core), par: 16 (over y_hi, z).
Axes of the slice: x: 4, y: 4 (y_hi: 2, y_lo: 2; y = y_hi * 2 + y_lo), z: 8, core: 2. Of those that a mesh axis runs over, the one named last changes fastest.
Arguments:
- partials: bfloat16 [16, 3, 128, 8192], P('arc', None, 'par'), may hold values from -6 to 6
- epoch_index: int32 [16, 128], P('arc'), may hold values from 0 to 511, as said below
- whitening: float32 [16, 3, 128, 128], P('arc'), may hold values from -2 to 2, as said below
Outputs:
- normal_matrix: float32 [8192, 8192], P('arc', 'par')
Inputs may be any that keep to these rules, and one draw needn't show every extreme that they name: `epoch_index`: in each arc the epoch indices rise strictly; the first is 0 and the last is 511. `whitening`: each block is lower triangular with diagonal entries between 1 and 2.
All inputs are finite; a program needn't handle non-finite values.
Results may differ from a plain program's by a relative error of at most 0.0003.
Values may be sent and summed in bfloat16 or wider, within the bound.
A program may use at most 128 MiB of HBM per device.

v0:
```python
import math

import jax
import jax.numpy as jnp
from jax import lax
from jax.sharding import PartitionSpec as P

KERNEL_GAIN = 8.0


def from_root(block, axis, owner):
    block = jnp.where(lax.axis_index(axis) == owner, block, jnp.zeros_like(block))
    return lax.psum(block, axis)


def mixing_matrices(epoch_index, whitening, epochs, row_scale):
    times_arc = epoch_index.astype(jnp.float32) / jnp.float32(4 * epochs - 1)
    later_time = times_arc[:, :, None]
    earlier_time = times_arc[:, None, :]
    green_part = jnp.minimum(later_time, earlier_time) * (
        1.0 - jnp.maximum(later_time, earlier_time)
    )
    kernel = jnp.eye(epochs, dtype=jnp.float32)[None] + KERNEL_GAIN / epochs * green_part
    mixing = jnp.einsum("acij,ajk->acik", whitening, kernel, precision=lax.Precision.HIGHEST)
    return mixing * row_scale


def on_device(partials, epoch_index, whitening):
    arc_local = partials.shape[0]
    epochs = epoch_index.shape[1]
    param_count = partials.shape[3]
    arc_count = lax.axis_size("arc")
    par_count = lax.axis_size("par")
    total_arcs = arc_local * arc_count
    col_block = param_count // par_count
    row_block = param_count // arc_count
    row_scale = 1.0 / math.sqrt(3 * epochs * total_arcs)
    mixing = mixing_matrices(epoch_index, whitening, epochs, row_scale)
    columns = lax.all_to_all(partials, "par", split_axis=3, concat_axis=2, tiled=True)
    arc_position = lax.axis_index("arc")
    holder = arc_position * row_block // col_block
    gathered = jnp.einsum(
        "acij,acjk->acik", mixing, columns.astype(jnp.float32), precision=lax.Precision.HIGHEST
    )
    gathered = lax.all_gather(gathered, "arc", axis=0, tiled=True)
    row_data = from_root(gathered, "par", holder)
    row_flat = row_data.reshape(-1, row_block)
    col_flat = gathered.reshape(-1, col_block)
    return lax.dot_general(
        row_flat,
        col_flat,
        (((0,), (0,)), ((), ())),
        precision=lax.Precision.HIGHEST,
        preferred_element_type=jnp.float32,
    )


def solution(mesh):
    placed = (P("arc", None, "par", None), P("arc", None), P("arc", None, None, None))
    return jax.shard_map(
        on_device, mesh=mesh, in_specs=placed, out_specs=P("arc", "par"), check_vma=False
    )
```

profile of v0, /device:TPU:1, one launch (start us, length us, event | category | flops | bytes accessed | tf_op | source)
XLA Modules:
  0.0 480.0 jit_solution(4543148357410827872)
XLA Ops:
  6.5 0.0 copy-start
  6.5 0.0 copy-start.1
  6.5 9.5 %copy.5 = bf16[1,3,8,8192]{2,1,0,3:T(4,128)(2,1)} copy(bf16[1,3,8,8192]{3,2,1,0:T(8,128)(2,1)} %param.3) | data formatting | bytes 786432 | tf_op args[0]
  16.1 13.6 %reshape.224 = bf16[16,2,6144]{2,1,0:T(2,128)(2,1)} reshape(bf16[8192,1,3,8]{3,2,1,0:T(4,128)(2,1)} %bitcast.30) | data formatting | bytes 786432
  29.7 11.7 %all-to-all-start = ((bf16[16,2,6144]{2,1,0:T(2,128)(2,1)}), bf16[16,2,6144]{2,1,0:T(2,128)(2,1)S(1)}, u32[]{:S(2)}, u32[]{:S(2)}) async-start(bf16[16,2,6144]{2,1,0:T(2,128)(2,1)} %reshape.224), calls=%async_computation | async-start | bytes 786432 | tf_op jit(solution)/shard_map/all_to_all | solution.py:39
  41.4 0.0 all-gather.3.cloned.1.call-start
  41.5 0.0 copy-done.1
  41.5 0.2 fusion.4
  41.7 0.0 copy-done
  41.7 0.3 fusion
  42.0 11.6 %all-to-all-done = bf16[16,2,6144]{2,1,0:T(2,128)(2,1)S(1)} async-done(((bf16[16,2,6144]{2,1,0:T(2,128)(2,1)}), bf16[16,2,6144]{2,1,0:T(2,128)(2,1)S(1)}, u32[]{:S(2)}, u32[]{:S(2)}) %all-to-all-start) | async-done | bytes 393248 | tf_op jit(solution)/shard_map/all_to_all | solution.py:39
  53.7 10.7 %reshape.225 = bf16[8192,1,3,8]{3,2,1,0:T(4,128)(2,1)} reshape(bf16[16,2,6144]{2,1,0:T(2,128)(2,1)S(1)} %all-to-all-done) | data formatting | bytes 786432
  64.3 10.4 %copy.6 = bf16[1,3,8,16,512]{4,2,3,1,0:T(8,128)(2,1)S(1)} copy(bf16[1,3,8,16,512]{2,1,4,3,0:T(4,128)(2,1)} %bitcast.29) | data formatting | bytes 786432 | tf_op jit(solution)/shard_map/all_to_all | solution.py:39
  74.8 1.4 fusion.1
  76.1 0.0 all-gather.3.cloned.1.call-update
  76.2 0.0 all-reduce.2.cloned.1.call-start
  76.2 73.7 %all-gather.3.cloned.1.call-done = f32[48,128,512]{2,1,0:T(8,128)} async-done(((f32[3,128,512]{2,1,0:T(8,128)}), f32[48,128,512]{2,1,0:T(8,128)}) %all-gather.3.cloned.1.call-update) | async-done | bytes 12582928 | tf_op jit(solution)/shard_map/all_gather | solution.py:45
  149.9 7.3 %broadcast_select_fusion = f32[16,3,128,512]{3,2,1,0:T(8,128)} fusion(f32[16,3,128,512]{3,2,1,0:T(8,128)} %bitcast.27, pred[]{:T(512)S(6)} %eq.21), kind=kLoop, calls=%fused_computation | loop fusion | flops 3145728 | bytes 25165824 | tf_op jit(solution)/shard_map/jit(_where)/select_n | solution.py:12
  157.2 0.0 all-reduce.2.cloned.1.call-update
  157.3 291.5 %all-reduce.2.cloned.1.call-done = f32[16,3,128,512]{3,2,1,0:T(8,128)} async-done(((f32[16,3,128,512]{3,2,1,0:T(8,128)}), f32[16,3,128,512]{3,2,1,0:T(8,128)}) %all-reduce.2.cloned.1.call-update) | async-done | bytes 12582928 | tf_op jit(solution)/shard_map/psum | solution.py:13
  448.8 24.4 %convolution_bitcast_fusion = f32[512,512]{1,0:T(8,128)} fusion(f32[16,3,128,512]{3,2,1,0:T(8,128)} %all-reduce.2.cloned.1.call-done, f32[16,3,128,512]{3,2,1,0:T(8,128)} %bitcast.28), kind=kOutput, calls=%fused_computation.1 | convolution fusion | flops 19327352832 | bytes 26214400 | tf_op jit(solution)/shard_map/dot_general | solution.py:49
  (1 shorter events, 0.0 us)
Async XLA Ops:
  6.5 35.2 %copy-start = (f32[1,3,128,128]{3,2,1,0:T(8,128)S(1)}, f32[1,3,128,128]{3,2,1,0:T(8,128)}, u32[]{:S(2)}) copy-start(f32[1,3,128,128]{3,2,1,0:T(8,128)} %param.5) | copy-start | bytes 589828
  6.5 34.9 %copy-start.1 = (s32[1,128]{1,0:T(1,128)S(1)}, s32[1,128]{1,0:T(1,128)}, u32[]{:S(2)}) copy-start(s32[1,128]{1,0:T(1,128)} %param.4) | copy-start | bytes 1540
  29.7 24.0 %all-to-all-start = ((bf16[16,2,6144]{2,1,0:T(2,128)(2,1)}), bf16[16,2,6144]{2,1,0:T(2,128)(2,1)S(1)}, u32[]{:S(2)}, u32[]{:S(2)}) async-start(bf16[16,2,6144]{2,1,0:T(2,128)(2,1)} %reshape.224), calls=%async_computation | async-start | bytes 786432 | tf_op jit(solution)/shard_map/all_to_all | solution.py:39
  41.4 108.5 %all-gather.3.cloned.1.call-start = ((), (), s32[]{:S(2)}) async-start(), calls=%async_computation.2 | async-start | bytes 13369344 | tf_op jit(solution)/shard_map/all_gather | solution.py:45
  76.2 372.6 %all-reduce.2.cloned.1.call-start = ((), (), s32[]{:S(2)}) async-start(), calls=%async_computation.1 | async-start | bytes 25165824 | tf_op jit(solution)/shard_map/psum | solution.py:13
Sparse Core Ops, SparseCore 0:
  76.3 73.5 all-gather.2
  157.4 291.3 all-reduce.1
where the time goes:
time: 482 us; the launch traced here: 480 us
  waiting for transfers between devices  377 us (78%)
  local copies, waits for them, and re-layouts  44.2 us (9%)
  matrix products  26.1 us (5%)
  between operations  13.5 us (3%)
  starting transfers between devices  11.8 us (2%)
  other arithmetic  7.55 us (2%)
    psum x1, waiting for transfers between devices, from_root(): return lax.psum(block, axis)  292 us
    all_gather x1, waiting for transfers between devices, on_device(): gathered = lax.all_gather(gathered, 'arc', axis=0, tiled=True)  73.7 us
    unnamed x7, local copies, waits for them, and re-layouts  33.8 us
    dot_general x1, matrix products, on_device(): lax.dot_general(row_flat, col_flat, (((0,), (0,)), ((), ())), precision=l...  24.4 us
    all_to_all x1, starting transfers between devices, on_device(): lax.all_to_all(partials, 'par', split_axis=3, concat_axis=2, tiled=True)  11.7 us
    all_to_all x1, waiting for transfers between devices, on_device(): lax.all_to_all(partials, 'par', split_axis=3, concat_axis=2, tiled=True)  11.6 us
    all_to_all x1, local copies, waits for them, and re-layouts, on_device(): lax.all_to_all(partials, 'par', split_axis=3, concat_axis=2, tiled=True)  10.4 us
  transfers between devices with their start and end apart: 3, of which 3 were waited for; matrix products, arithmetic and copies ran while one was open for 0% of the time, Pallas kernels for 0%

commit v1 on v0

v1 whole, which is shorter than its diff:
```python
import math

import jax
import jax.numpy as jnp
from jax import lax
from jax.experimental import pallas as pl
from jax.experimental.pallas import tpu as pltpu
from jax.sharding import PartitionSpec as P

KERNEL_GAIN = 8.0
MESH = pl.DeviceIdType.MESH
EARLY = 8
N_SEM = 80


def kernel(part_ref, epoch_ref, white_ref, out_ref, blocks, rows, cols, mixers, q_all, send_sem, recv_sem, bulk_send, bulk_recv):
    a = lax.axis_index("arc")
    p = lax.axis_index("par")
    x, yl, core = a // 4, (a // 2) % 2, a % 2
    yh, z = p // 8, p % 8
    other_core = (x * 4 + yl * 2 + 1 - core, p)
    yl_partner = (x * 4 + (1 - yl) * 2 + core, p)
    yh_partner = (a, (1 - yh) * 8 + z)

    def arc_at(dx, same_yl, same_core):
        return (
            ((x + dx + 4) % 4) * 4
            + (yl if same_yl else 1 - yl) * 2
            + (core if same_core else 1 - core)
        )

    def par_at(same_yh, dz):
        return (yh if same_yh else 1 - yh) * 8 + (z + dz + 8) % 8

    barrier = pltpu.get_barrier_semaphore()

    def greet(k, _):
        pl.semaphore_signal(barrier, inc=1, device_id=((a + k) % 16, p), device_id_type=MESH)
        pl.semaphore_signal(barrier, inc=1, device_id=(a, (p + k) % 16), device_id_type=MESH)
        return 0

    lax.fori_loop(1, 16, greet, 0)

    for c in range(3):
        for b in range(16):
            piece = part_ref[0, c, :, b * 512 : (b + 1) * 512].astype(jnp.float32)
            unit = jnp.concatenate([piece[:, :256], piece[:, 256:]], axis=0)
            blocks[b, c * 16 : (c + 1) * 16, :] = unit.astype(jnp.bfloat16)

    pl.semaphore_wait(barrier, 30)

    def send_rows(k, _):
        b = (a + k) % 16
        pltpu.make_async_remote_copy(
            src_ref=blocks.at[b], dst_ref=rows.at[p, a], send_sem=bulk_send.at[0], recv_sem=bulk_recv.at[0],
            device_id=(b, p), device_id_type=MESH,
        ).start()
        return 0

    def send_cols(k, _):
        b = (p + k) % 16
        pltpu.make_async_remote_copy(
            src_ref=blocks.at[b], dst_ref=cols.at[a, p], send_sem=bulk_send.at[1], recv_sem=bulk_recv.at[1],
            device_id=(a, b), device_id_type=MESH,
        ).start()
        return 0

    lax.fori_loop(1, 16, send_rows, 0)
    lax.fori_loop(1, 16, send_cols, 0)
    rows[p, a] = blocks[a]
    cols[a, p] = blocks[p]

    row_scale = 1.0 / math.sqrt(6144)
    times = epoch_ref[...].astype(jnp.float32) / jnp.float32(511)
    later = jnp.broadcast_to(times, (128, 128))
    earlier = jnp.transpose(later)
    i = lax.broadcasted_iota(jnp.int32, (128, 128), 0)
    j = lax.broadcasted_iota(jnp.int32, (128, 128), 1)
    eye = jnp.where(i == j, 1.0, 0.0).astype(jnp.float32)
    green = jnp.minimum(later, earlier) * (1.0 - jnp.maximum(later, earlier))
    integral = eye + KERNEL_GAIN / 128 * green
    for c in range(3):
        m = jnp.dot(white_ref[0, c], integral, precision=lax.Precision.HIGHEST, preferred_element_type=jnp.float32) * row_scale
        g = jnp.dot(jnp.transpose(m), m, precision=lax.Precision.HIGHEST, preferred_element_type=jnp.float32)
        high = g.astype(jnp.bfloat16)
        low = (g - high.astype(jnp.float32)).astype(jnp.bfloat16)
        mixers[a, c * 128 : (c + 1) * 128, :] = jnp.concatenate([high, low], axis=1)

    counter = [0]
    started = []

    class Link:
        def __init__(self, target, src, landing):
            self.n = counter[0]
            counter[0] += 1
            self.target, self.src, self.landing = target, src, landing

        def start(self):
            self.copy = pltpu.make_async_remote_copy(
                src_ref=self.src, dst_ref=self.src, send_sem=send_sem.at[self.n], recv_sem=recv_sem.at[self.n],
                device_id=self.target, device_id_type=MESH,
            )
            self.copy.start()
            started.append(self.copy)

        def arrived(self):
            pltpu.make_async_remote_copy(
                src_ref=self.landing, dst_ref=self.landing, send_sem=send_sem.at[self.n], recv_sem=recv_sem.at[self.n],
                device_id=self.target, device_id_type=MESH,
            ).wait_recv()

    tasks = []

    def at(time, act):
        tasks.append((time, len(tasks), act))

    def row_part(part, dz, half=None):
        same = part != "E1"
        lo, n = (0, EARLY) if part in ("E0", "E1") else (EARLY, 16 - EARLY)
        if half is not None:
            n1 = n // 2
            lo, n = (lo, n1) if half == 0 else (lo + n1, n - n1)
        return rows.at[par_at(same, dz), pl.ds(lo, n)]

    parts = ("L", "E0", "E1")
    z_to = {1: (a, par_at(True, 1)), -1: (a, par_at(True, -1))}
    ring = {}
    for step in range(1, 5):
        for part in parts:
            for d in (1, -1):
                half = None if step < 4 else (0 if d == 1 else 1)
                ring[step, part, d] = Link(
                    z_to[d], row_part(part, -d * (step - 1), half), row_part(part, -d * step, half)
                )
    cross_early = Link(yh_partner, rows.at[p, pl.ds(0, EARLY)], rows.at[par_at(False, 0), pl.ds(0, EARLY)])
    late = pl.ds(EARLY, 16 - EARLY)
    cross_late = {
        dz: Link(yh_partner, rows.at[par_at(True, dz), late], rows.at[par_at(False, dz), late])
        for dz in (0, 1, -1, 2, -2, 3, -3, 4)
    }

    def rows_ready():
        pltpu.make_async_copy(rows.at[p, pl.ds(0, 15)], rows.at[p, pl.ds(0, 15)], bulk_recv.at[0]).wait()
        cross_early.start()
        for part in ("L", "E0"):
            for d in (1, -1):
                ring[1, part, d].start()
        cross_late[0].start()

    at(5, rows_ready)

    def early_crossed():
        cross_early.arrived()
        for d in (1, -1):
            ring[1, "E1", d].start()

    at(9.6, early_crossed)

    def ring_arrival(step, part, d):
        ring[step, part, d].arrived()
        if step < 4:
            ring[step + 1, part, d].start()
        if part == "L" and step < 4:
            cross_late[-d * step].start()

    for step in range(1, 5):
        for n, part in enumerate(parts):
            for d in (1, -1):
                time = 5 + 4.2 * (1 + 3 * (step - 1) + n) if step < 4 else 43 + 2.1 * (n + 1)
                at(time, lambda s=step, q=part, d=d: ring_arrival(s, q, d))

    def last_late():
        cross_late[4].start()

    at(45.2, last_late)

    def gather_over_arc(buf, extent, time, first):
        def piece(arc, half=None):
            if half is None:
                return buf.at[arc]
            n = extent // 2
            return buf.at[arc, pl.ds(half * n, n)]

        x_to = {1: (arc_at(1, True, True), p), -1: (arc_at(-1, True, True), p)}
        to_yl = Link(yl_partner, piece(a), piece(arc_at(0, False, True)))
        hops, cores = {}, {}
        for mine in (True, False):
            for d in (1, -1):
                hops[1, mine, d] = Link(x_to[d], piece(arc_at(0, mine, True)), piece(arc_at(-d, mine, True)))
                half = 0 if d == 1 else 1
                hops[2, mine, d] = Link(x_to[d], piece(arc_at(-d, mine, True), half), piece(arc_at(2, mine, True), half))
            cores[0, mine] = Link(other_core, piece(arc_at(0, mine, True)), piece(arc_at(0, mine, False)))
            for d in (1, -1):
                cores[1, mine, d] = Link(other_core, piece(arc_at(-d, mine, True)), piece(arc_at(-d, mine, False)))
                half = 0 if d == 1 else 1
                cores[2, mine, d] = Link(other_core, piece(arc_at(2, mine, True), half), piece(arc_at(2, mine, False), half))

        def begin():
            first()
            to_yl.start()
            for d in (1, -1):
                hops[1, True, d].start()
            cores[0, True].start()

        def yl_arrival():
            to_yl.arrived()
            for d in (1, -1):
                hops[1, False, d].start()
            cores[0, False].start()

        def hop_arrival(dist, mine, d):
            hops[dist, mine, d].arrived()
            if dist == 1:
                hops[2, mine, d].start()
            cores[dist, mine, d].start()

        at(time["begin"], begin)
        at(time["yl"], yl_arrival)
        for mine in (True, False):
            for dist in (1, 2):
                for d in (1, -1):
                    at(time[dist, mine], lambda s=dist, m=mine, d=d: hop_arrival(s, m, d))

        def wait_group(dist, mine):
            if dist == 0:
                cores[0, mine].arrived()
            else:
                for d in (1, -1):
                    cores[dist, mine, d].arrived()

        return wait_group

    wait_g = gather_over_arc(
        mixers, 384,
        {"begin": 4, "yl": 8, (1, True): 8.5, (1, False): 13, (2, True): 15, (2, False): 17.5},
        lambda: None,
    )

    def cols_ready():
        pltpu.make_async_copy(cols.at[a, pl.ds(0, 15)], cols.at[a, pl.ds(0, 15)], bulk_recv.at[1]).wait()

    wait_c = gather_over_arc(
        cols, 16,
        {"begin": 10, "yl": 19, (1, True): 24.5, (1, False): 33, (2, True): 37.1, (2, False): 41.3},
        cols_ready,
    )

    def mix(arc):
        for c in range(3):
            unit = cols[arc, :, c * 16 : (c + 1) * 16, :].astype(jnp.float32).reshape(16, 2, 8, 256)
            b = jnp.concatenate([unit[:, 0].reshape(128, 256), unit[:, 1].reshape(128, 256)], axis=1).astype(jnp.bfloat16)
            q = jnp.dot(
                mixers[arc, c * 128 : (c + 1) * 128, :], jnp.concatenate([b, b], axis=0), preferred_element_type=jnp.float32
            )
            q_all[:, arc * 3 + c] = q.reshape(16, 8, 512)

    def mix_group(dist, mine):
        waits = []
        if dist < 2:
            wait_g(dist, mine), wait_c(dist, mine)
        else:
            wait_g(dist, mine), wait_c(dist, mine)
        yl_of = yl if mine else 1 - yl
        if dist == 1:
            def body(k, _):
                dx = (k // 2) * 2 - 1
                mix(((x + dx + 4) % 4) * 4 + yl_of * 2 + k % 2)
                return 0
            lax.fori_loop(0, 4, body, 0)
        else:
            def body(k, _):
                mix(((x + dist) % 4) * 4 + yl_of * 2 + k)
                return 0
            lax.fori_loop(0, 2, body, 0)

    at(20, lambda: mix_group(0, True))
    at(22, lambda: mix_group(0, False))
    at(28, lambda: mix_group(1, True))
    at(35, lambda: mix_group(1, False))
    at(38.5, lambda: mix_group(2, True))
    at(42.5, lambda: mix_group(2, False))

    def accumulate(par, first=False):
        unit = rows[par].astype(jnp.float32).reshape(16, 3, 2, 8, 256)
        b = jnp.concatenate([unit[:, :, 0].reshape(384, 256), unit[:, :, 1].reshape(384, 256)], axis=1).astype(jnp.bfloat16)
        bt = jnp.transpose(b)
        q = q_all[par].reshape(384, 512)
        high = q.astype(jnp.bfloat16)
        low = (q - high.astype(jnp.float32)).astype(jnp.bfloat16)
        term = jnp.dot(
            jnp.concatenate([bt, bt], axis=1), jnp.concatenate([high, low], axis=0), preferred_element_type=jnp.float32
        )
        out_ref[...] += term

    def accumulate_group(dist):
        if dist == 0:
            cross_late[0].arrived()
            out_ref[...] = jnp.zeros_like(out_ref)
        elif dist < 4:
            cross_late[dist].arrived()
            cross_late[-dist].arrived()
        else:
            cross_late[4].arrived()
        if dist in (0, 4):
            def body(k, _):
                accumulate(k * 8 + (z + dist) % 8)
                return 0
            lax.fori_loop(0, 2, body, 0)
        else:
            def body(k, _):
                dz = dist * ((k // 2) * 2 - 1)
                accumulate((k % 2) * 8 + (z + dz + 8) % 8)
                return 0
            lax.fori_loop(0, 4, body, 0)

    at(42.6, lambda: accumulate_group(0))
    at(43.5, lambda: accumulate_group(1))
    at(46, lambda: accumulate_group(2))
    at(49.4, lambda: accumulate_group(3))
    at(52, lambda: accumulate_group(4))

    for _, _, act in sorted(tasks, key=lambda t: t[:2]):
        act()

    assert counter[0] <= N_SEM
    for n in (0, 1):
        pltpu.make_async_copy(blocks.at[pl.ds(0, 15)], blocks.at[pl.ds(0, 15)], bulk_send.at[n]).wait()
    for copy in started:
        copy.wait_send()


def on_device(partials, epoch_index, whitening):
    vmem = pl.BlockSpec(memory_space=pltpu.VMEM)
    return pl.pallas_call(
        kernel,
        out_shape=jax.ShapeDtypeStruct((512, 512), jnp.float32),
        in_specs=[vmem, vmem, vmem],
        out_specs=vmem,
        scratch_shapes=[
            pltpu.VMEM((16, 48, 256), jnp.bfloat16),
            pltpu.VMEM((16, 16, 48, 256), jnp.bfloat16),
            pltpu.VMEM((16, 16, 48, 256), jnp.bfloat16),
            pltpu.VMEM((16, 384, 256), jnp.bfloat16),
            pltpu.VMEM((16, 48, 8, 512), jnp.float32),
            pltpu.SemaphoreType.DMA((N_SEM,)),
            pltpu.SemaphoreType.DMA((N_SEM,)),
            pltpu.SemaphoreType.DMA((2,)),
            pltpu.SemaphoreType.DMA((2,)),
        ],
        compiler_params=pltpu.CompilerParams(
            collective_id=0, has_side_effects=True, vmem_limit_bytes=56 * 2**20
        ),
    )(partials, epoch_index, whitening)


def solution(mesh):
    placed = (P("arc", None, "par", None), P("arc", None), P("arc", None, None, None))
    return jax.shard_map(
        on_device, mesh=mesh, in_specs=placed, out_specs=P("arc", "par"), check_vma=False
    )
```

time: 482 us -> 89.9 us (0.19)
  waiting for transfers between devices: 377 us -> 0 us
  Pallas kernels: 0 us -> 87.5 us
  local copies, waits for them, and re-layouts: 44.2 us -> 2.26 us
  matrix products: 26.1 us -> 0 us
  between operations: 13.5 us -> 0.01 us
  starting transfers between devices: 11.8 us -> 0 us
  other arithmetic: 7.55 us -> 0 us
    psum x1 -> x0, waiting for transfers between devices: 292 us -> none  [from_root(): return lax.psum(block, axis)]
    pallas_call x0 -> x1, Pallas kernels: none -> 87.5 us  [on_device(): pl.pallas_call(kernel, out_shape=jax.ShapeDtypeStruct((512, 512), jnp.flo...]
    all_gather x1 -> x0, waiting for transfers between devices: 73.7 us -> none  [on_device(): gathered = lax.all_gather(gathered, 'arc', axis=0, tiled=True)]
    unnamed x7 -> x1, local copies, waits for them, and re-layouts: 33.8 us -> 2.26 us
    dot_general x3 -> x0, matrix products: 26.1 us -> none  [the longest x1 24.4 us: on_device(): lax.dot_general(row_flat, col_flat, (((0,), (0,)), ((), ())), precision=l...]
    all_to_all x1 -> x0, starting transfers between devices: 11.7 us -> none  [on_device(): lax.all_to_all(partials, 'par', split_axis=3, concat_axis=2, tiled=True)]
    all_to_all x1 -> x0, waiting for transfers between devices: 11.6 us -> none  [on_device(): lax.all_to_all(partials, 'par', split_axis=3, concat_axis=2, tiled=True)]
    all_to_all x1 -> x0, local copies, waits for them, and re-layouts: 10.4 us -> none  [on_device(): lax.all_to_all(partials, 'par', split_axis=3, concat_axis=2, tiled=True)]
  transfers between devices with their start and end apart: 3 -> 0, of which waited for: 3 -> 0; matrix products, arithmetic and copies ran while one was open for 0% -> 0% of each run, Pallas kernels for 0% -> 0%
where the time goes in v1:
time: 89.9 us; the launch traced here: 89.7 us
  Pallas kernels  87.5 us (97%)
  local copies, waits for them, and re-layouts  2.26 us (3%)
    pallas_call x1, Pallas kernels, on_device(): pl.pallas_call(kernel, out_shape=jax.ShapeDtypeStruct((512, 512), jnp.flo...  87.5 us
    unnamed x1, local copies, waits for them, and re-layouts  2.26 us

profile of v1, /device:TPU:1, one launch (start us, length us, event | category | flops | bytes accessed | tf_op | source)
XLA Modules:
  0.0 89.7 jit_solution(12513370661692913848)
XLA Ops:
  0.0 87.5 %shard_map.37 = f32[512,512]{1,0:T(8,128)} custom-call(bf16[1,3,8,8192]{3,2,1,0:T(8,128)(2,1)} %part_ref.1, s32[1,128]{1,0:T(1,128)} %epoch_ref.1, f32[1,3,128,128]{3,2,1,0:T(8,128)} %white_ref.1), custom_call_target="tpu_custom_call" | custom-call | tf_op jit(solution)/shard_map/pallas_call | solution.py:334
  87.5 2.3 %copy.5 = f32[512,512]{1,0:T(8,128)} copy(f32[512,512]{1,0:T(8,128)} %shard_map.37) | data formatting | bytes 2097152

commit v2 on v1

--- a/solution.py
+++ b/solution.py
@@ -11,6 +11,19 @@
 MESH = pl.DeviceIdType.MESH
 EARLY = 8
 N_SEM = 80
+ORDER = (
+    ("G", "begin"), ("C", "begin"), ("G", 1, True, 1), ("G", 1, True, -1), "rows", ("G", 2, True, 1),
+    ("G", "yl"), ("mix", 0, True), ("G", 2, True, -1), ("z", 1, "E0", -1), ("z", 1, "E0", 1),
+    ("z", 1, "L", -1), ("z", 1, "L", 1), ("G", 1, False, 1), "early", ("G", 1, False, -1), ("C", 1, True, 1),
+    ("C", 1, True, -1), ("G", 2, False, -1), ("G", 2, False, 1), ("mix", 1, True), ("z", 2, "L", 1),
+    ("z", 2, "L", -1), ("z", 2, "E0", 1), ("C", 2, True, -1), ("z", 1, "E1", 1), ("z", 2, "E0", -1),
+    ("C", 2, True, 1), ("z", 1, "E1", -1), ("mix", 2, True), ("C", "yl"), ("z", 3, "L", 1), ("z", 3, "L", -1),
+    ("mix", 0, False), ("z", 3, "E0", 1), ("z", 2, "E1", 1), ("z", 2, "E1", -1), ("z", 3, "E0", -1),
+    ("C", 1, False, 1), ("C", 1, False, -1), ("mix", 1, False), ("z", 4, "L", -1), ("z", 4, "L", 1), "last",
+    ("C", 2, False, 1), ("C", 2, False, -1), ("mix", 2, False), ("acc", 0), ("z", 3, "E1", -1),
+    ("z", 3, "E1", 1), ("acc", 1), ("acc", 3), ("z", 4, "E0", -1), ("z", 4, "E1", -1), ("z", 4, "E0", 1),
+    ("z", 4, "E1", 1), ("acc", 4), ("acc", 2),
+)
 
 
 def kernel(part_ref, epoch_ref, white_ref, out_ref, blocks, rows, cols, mixers, q_all, send_sem, recv_sem, bulk_send, bulk_recv):
@@ -109,10 +122,10 @@
                 device_id=self.target, device_id_type=MESH,
             ).wait_recv()
 
-    tasks = []
-
-    def at(time, act):
-        tasks.append((time, len(tasks), act))
+    tasks = {}
+
+    def at(key, act):
+        tasks[key] = act
 
     def row_part(part, dz, half=None):
         same = part != "E1"
@@ -147,14 +160,14 @@
                 ring[1, part, d].start()
         cross_late[0].start()
 
-    at(5, rows_ready)
+    at("rows", rows_ready)
 
     def early_crossed():
         cross_early.arrived()
         for d in (1, -1):
             ring[1, "E1", d].start()
 
-    at(9.6, early_crossed)
+    at("early", early_crossed)
 
     def ring_arrival(step, part, d):
         ring[step, part, d].arrived()
@@ -164,17 +177,16 @@
             cross_late[-d * step].start()
 
     for step in range(1, 5):
-        for n, part in enumerate(parts):
-            for d in (1, -1):
-                time = 5 + 4.2 * (1 + 3 * (step - 1) + n) if step < 4 else 43 + 2.1 * (n + 1)
-                at(time, lambda s=step, q=part, d=d: ring_arrival(s, q, d))
+        for part in parts:
+            for d in (1, -1):
+                at(("z", step, part, d), lambda s=step, q=part, d=d: ring_arrival(s, q, d))
 
     def last_late():
         cross_late[4].start()
 
-    at(45.2, last_late)
-
-    def gather_over_arc(buf, extent, time, first):
+    at("last", last_late)
+
+    def gather_over_arc(name, buf, extent, first):
         def piece(arc, half=None):
             if half is None:
                 return buf.at[arc]
@@ -214,12 +226,12 @@
                 hops[2, mine, d].start()
             cores[dist, mine, d].start()
 
-        at(time["begin"], begin)
-        at(time["yl"], yl_arrival)
+        at((name, "begin"), begin)
+        at((name, "yl"), yl_arrival)
         for mine in (True, False):
             for dist in (1, 2):
                 for d in (1, -1):
-                    at(time[dist, mine], lambda s=dist, m=mine, d=d: hop_arrival(s, m, d))
+                    at((name, dist, mine, d), lambda s=dist, m=mine, d=d: hop_arrival(s, m, d))
 
         def wait_group(dist, mine):
             if dist == 0:
@@ -230,20 +242,12 @@
 
         return wait_group
 
-    wait_g = gather_over_arc(
-        mixers, 384,
-        {"begin": 4, "yl": 8, (1, True): 8.5, (1, False): 13, (2, True): 15, (2, False): 17.5},
-        lambda: None,
-    )
+    wait_g = gather_over_arc("G", mixers, 384, lambda: None)
 
     def cols_ready():
         pltpu.make_async_copy(cols.at[a, pl.ds(0, 15)], cols.at[a, pl.ds(0, 15)], bulk_recv.at[1]).wait()
 
-    wait_c = gather_over_arc(
-        cols, 16,
-        {"begin": 10, "yl": 19, (1, True): 24.5, (1, False): 33, (2, True): 37.1, (2, False): 41.3},
-        cols_ready,
-    )
+    wait_c = gather_over_arc("C", cols, 16, cols_ready)
 
     def mix(arc):
         for c in range(3):
@@ -255,11 +259,8 @@
             q_all[:, arc * 3 + c] = q.reshape(16, 8, 512)
 
     def mix_group(dist, mine):
-        waits = []
-        if dist < 2:
-            wait_g(dist, mine), wait_c(dist, mine)
-        else:
-            wait_g(dist, mine), wait_c(dist, mine)
+        wait_g(dist, mine)
+        wait_c(dist, mine)
         yl_of = yl if mine else 1 - yl
         if dist == 1:
             def body(k, _):
@@ -273,14 +274,11 @@
                 return 0
             lax.fori_loop(0, 2, body, 0)
 
-    at(20, lambda: mix_group(0, True))
-    at(22, lambda: mix_group(0, False))
-    at(28, lambda: mix_group(1, True))
-    at(35, lambda: mix_group(1, False))
-    at(38.5, lambda: mix_group(2, True))
-    at(42.5, lambda: mix_group(2, False))
-
-    def accumulate(par, first=False):
+    for dist in range(3):
+        for mine in (True, False):
+            at(("mix", dist, mine), lambda s=dist, m=mine: mix_group(s, m))
+
+    def accumulate(par):
         unit = rows[par].astype(jnp.float32).reshape(16, 3, 2, 8, 256)
         b = jnp.concatenate([unit[:, :, 0].reshape(384, 256), unit[:, :, 1].reshape(384, 256)], axis=1).astype(jnp.bfloat16)
         bt = jnp.transpose(b)
@@ -313,14 +311,12 @@
                 return 0
             lax.fori_loop(0, 4, body, 0)
 
-    at(42.6, lambda: accumulate_group(0))
-    at(43.5, lambda: accumulate_group(1))
-    at(46, lambda: accumulate_group(2))
-    at(49.4, lambda: accumulate_group(3))
-    at(52, lambda: accumulate_group(4))
-
-    for _, _, act in sorted(tasks, key=lambda t: t[:2]):
-        act()
+    for dist in range(5):
+        at(("acc", dist), lambda s=dist: accumulate_group(s))
+
+    assert sorted(map(str, tasks)) == sorted(map(str, ORDER))
+    for key in ORDER:
+        tasks[key]()
 
     assert counter[0] <= N_SEM
     for n in (0, 1):

time: 89.9 us -> 87.4 us (0.972)
  Pallas kernels: 87.5 us -> 85 us
    pallas_call x1, Pallas kernels: 87.5 us -> 85 us  [on_device(): pl.pallas_call(kernel, out_shape=jax.ShapeDtypeStruct((512, 512), jnp.flo...]
where the time goes in v2:
time: 87.4 us; the launch traced here: 87.3 us
  Pallas kernels  85 us (97%)
  local copies, waits for them, and re-layouts  2.26 us (3%)
    pallas_call x1, Pallas kernels, on_device(): pl.pallas_call(kernel, out_shape=jax.ShapeDtypeStruct((512, 512), jnp.flo...  85 us
    unnamed x1, local copies, waits for them, and re-layouts  2.26 us

profile of v2, /device:TPU:1, one launch (start us, length us, event | category | flops | bytes accessed | tf_op | source)
XLA Modules:
  0.0 87.3 jit_solution(9525078648163446672)
XLA Ops:
  0.0 85.0 %shard_map.37 = f32[512,512]{1,0:T(8,128)} custom-call(bf16[1,3,8,8192]{3,2,1,0:T(8,128)(2,1)} %part_ref.1, s32[1,128]{1,0:T(1,128)} %epoch_ref.1, f32[1,3,128,128]{3,2,1,0:T(8,128)} %white_ref.1), custom_call_target="tpu_custom_call" | custom-call | tf_op jit(solution)/shard_map/pallas_call | solution.py:330
  85.0 2.3 %copy.5 = f32[512,512]{1,0:T(8,128)} copy(f32[512,512]{1,0:T(8,128)} %shard_map.37) | data formatting | bytes 2097152

commit v3 on v2

--- a/solution.py
+++ b/solution.py
@@ -11,22 +11,25 @@
 MESH = pl.DeviceIdType.MESH
 EARLY = 8
 N_SEM = 80
+GROUPS = ((-2, 1, 5), (-3, 6, 2), (4, 1, 1))
 ORDER = (
-    ("G", "begin"), ("C", "begin"), ("G", 1, True, 1), ("G", 1, True, -1), "rows", ("G", 2, True, 1),
-    ("G", "yl"), ("mix", 0, True), ("G", 2, True, -1), ("z", 1, "E0", -1), ("z", 1, "E0", 1),
-    ("z", 1, "L", -1), ("z", 1, "L", 1), ("G", 1, False, 1), "early", ("G", 1, False, -1), ("C", 1, True, 1),
-    ("C", 1, True, -1), ("G", 2, False, -1), ("G", 2, False, 1), ("mix", 1, True), ("z", 2, "L", 1),
-    ("z", 2, "L", -1), ("z", 2, "E0", 1), ("C", 2, True, -1), ("z", 1, "E1", 1), ("z", 2, "E0", -1),
-    ("C", 2, True, 1), ("z", 1, "E1", -1), ("mix", 2, True), ("C", "yl"), ("z", 3, "L", 1), ("z", 3, "L", -1),
-    ("mix", 0, False), ("z", 3, "E0", 1), ("z", 2, "E1", 1), ("z", 2, "E1", -1), ("z", 3, "E0", -1),
-    ("C", 1, False, 1), ("C", 1, False, -1), ("mix", 1, False), ("z", 4, "L", -1), ("z", 4, "L", 1), "last",
-    ("C", 2, False, 1), ("C", 2, False, -1), ("mix", 2, False), ("acc", 0), ("z", 3, "E1", -1),
-    ("z", 3, "E1", 1), ("acc", 1), ("acc", 3), ("z", 4, "E0", -1), ("z", 4, "E1", -1), ("z", 4, "E0", 1),
-    ("z", 4, "E1", 1), ("acc", 4), ("acc", 2),
+    "clear", ("G", "begin"), ("G", 1, True, 1), ("G", 1, True, -1), "rows", ("C", "begin"), ("mix", 0, True),
+    ("G", 2, True, 1), ("G", 2, True, -1), ("G", "yl"), "early", ("z", 1, "E0", 1), ("z", 1, "L", 1),
+    ("late", 0), ("z", 1, "L", -1), ("late", 1), ("G", 1, False, 1), ("G", 1, False, -1), ("C", 1, True, -1),
+    ("z", 1, "E0", -1), ("late", -1), ("C", 1, True, 1), ("mix", 1, True), ("G", 2, False, -1),
+    ("C", 2, True, -1), ("z", 1, "E1", -1), ("C", "yl"), ("C", 2, True, 1), ("z", 1, "E1", 1),
+    ("z", 2, "L", 1), ("late", -2), ("z", 2, "L", -1), ("late", 2), ("z", 2, "E0", 1), ("mix", 2, True),
+    ("turn", 0), ("turn", 1), ("G", 2, False, 1), ("mix", 0, False), ("z", 2, "E0", -1), ("C", 1, False, 1),
+    ("C", 1, False, -1), ("turn", -1), ("z", 2, "E1", 1), ("z", 2, "E1", -1), ("mix", 1, False),
+    ("z", 3, "L", -1), ("late", 3), ("z", 3, "L", 1), ("turn", 2), ("turn", -2), ("z", 3, "E0", -1),
+    ("late", -3), ("C", 2, False, 1), ("z", 3, "E0", 1), ("C", 2, False, -1), ("mix", 2, False),
+    ("sum", (-2, 1, 5)), ("z", 4, "L", -1), ("z", 3, "E1", -1), ("z", 4, "E0", -1), ("z", 4, "L", 1),
+    ("late", 4), ("z", 3, "E1", 1), ("turn", 3), ("z", 4, "E0", 1), ("z", 4, "E1", -1), ("turn", -3),
+    ("sum", (-3, 6, 2)), ("z", 4, "E1", 1), ("turn", 4), ("sum", (4, 1, 1)),
 )
 
 
-def kernel(part_ref, epoch_ref, white_ref, out_ref, blocks, rows, cols, mixers, q_all, send_sem, recv_sem, bulk_send, bulk_recv):
+def kernel(part_ref, epoch_ref, white_ref, out_ref, blocks, rows, cols, mixers, rows_t, q_high, q_low, send_sem, recv_sem, bulk_send, bulk_recv):
     a = lax.axis_index("arc")
     p = lax.axis_index("par")
     x, yl, core = a // 4, (a // 2) % 2, a % 2
@@ -158,7 +161,6 @@
         for part in ("L", "E0"):
             for d in (1, -1):
                 ring[1, part, d].start()
-        cross_late[0].start()
 
     at("rows", rows_ready)
 
@@ -173,18 +175,14 @@
         ring[step, part, d].arrived()
         if step < 4:
             ring[step + 1, part, d].start()
-        if part == "L" and step < 4:
-            cross_late[-d * step].start()
 
     for step in range(1, 5):
         for part in parts:
             for d in (1, -1):
                 at(("z", step, part, d), lambda s=step, q=part, d=d: ring_arrival(s, q, d))
 
-    def last_late():
-        cross_late[4].start()
-
-    at("last", last_late)
+    for dz in cross_late:
+        at(("late", dz), lambda dz=dz: cross_late[dz].start())
 
     def gather_over_arc(name, buf, extent, first):
         def piece(arc, half=None):
@@ -256,7 +254,10 @@
             q = jnp.dot(
                 mixers[arc, c * 128 : (c + 1) * 128, :], jnp.concatenate([b, b], axis=0), preferred_element_type=jnp.float32
             )
-            q_all[:, arc * 3 + c] = q.reshape(16, 8, 512)
+            q = jnp.swapaxes(q.reshape(2, 8, 8, 512), 0, 1).reshape(8, 16, 512)
+            high = q.astype(jnp.bfloat16)
+            q_high[:, arc * 3 + c] = high
+            q_low[:, arc * 3 + c] = (q - high.astype(jnp.float32)).astype(jnp.bfloat16)
 
     def mix_group(dist, mine):
         wait_g(dist, mine)
@@ -278,41 +279,41 @@
         for mine in (True, False):
             at(("mix", dist, mine), lambda s=dist, m=mine: mix_group(s, m))
 
-    def accumulate(par):
-        unit = rows[par].astype(jnp.float32).reshape(16, 3, 2, 8, 256)
-        b = jnp.concatenate([unit[:, :, 0].reshape(384, 256), unit[:, :, 1].reshape(384, 256)], axis=1).astype(jnp.bfloat16)
-        bt = jnp.transpose(b)
-        q = q_all[par].reshape(384, 512)
-        high = q.astype(jnp.bfloat16)
-        low = (q - high.astype(jnp.float32)).astype(jnp.bfloat16)
-        term = jnp.dot(
-            jnp.concatenate([bt, bt], axis=1), jnp.concatenate([high, low], axis=0), preferred_element_type=jnp.float32
-        )
-        out_ref[...] += term
-
-    def accumulate_group(dist):
-        if dist == 0:
-            cross_late[0].arrived()
-            out_ref[...] = jnp.zeros_like(out_ref)
-        elif dist < 4:
-            cross_late[dist].arrived()
-            cross_late[-dist].arrived()
-        else:
-            cross_late[4].arrived()
-        if dist in (0, 4):
-            def body(k, _):
-                accumulate(k * 8 + (z + dist) % 8)
-                return 0
-            lax.fori_loop(0, 2, body, 0)
-        else:
-            def body(k, _):
-                dz = dist * ((k // 2) * 2 - 1)
-                accumulate((k % 2) * 8 + (z + dz + 8) % 8)
-                return 0
-            lax.fori_loop(0, 4, body, 0)
-
-    for dist in range(5):
-        at(("acc", dist), lambda s=dist: accumulate_group(s))
+    def turn(dz):
+        cross_late[dz].arrived()
+        at_z = (z + dz + 8) % 8
+        halves = []
+        for h in range(2):
+            sides = [
+                rows[side * 8 + at_z].astype(jnp.float32).reshape(16, 3, 2, 8, 256)[:, :, h].reshape(48, 1, 8, 256)
+                for side in range(2)
+            ]
+            halves.append(jnp.concatenate(sides, axis=1).reshape(768, 256))
+        rows_t[at_z] = jnp.transpose(jnp.concatenate(halves, axis=1).astype(jnp.bfloat16))
+
+    def clear():
+        out_ref[...] = jnp.zeros_like(out_ref)
+
+    at("clear", clear)
+    for dz in cross_late:
+        at(("turn", dz), lambda dz=dz: turn(dz))
+
+    def accumulate(at_z):
+        left = rows_t[at_z]
+        right = jnp.concatenate([q_high[at_z].reshape(768, 512), q_low[at_z].reshape(768, 512)], axis=0)
+        out_ref[...] += jnp.dot(jnp.concatenate([left, left], axis=1), right, preferred_element_type=jnp.float32)
+
+    def accumulate_group(group):
+        first, stride, count = group
+
+        def body(k, _):
+            accumulate((z + first + stride * k + 8) % 8)
+            return 0
+
+        lax.fori_loop(0, count, body, 0)
+
+    for group in GROUPS:
+        at(("sum", group), lambda g=group: accumulate_group(g))
 
     assert sorted(map(str, tasks)) == sorted(map(str, ORDER))
     for key in ORDER:
@@ -337,7 +338,9 @@
             pltpu.VMEM((16, 16, 48, 256), jnp.bfloat16),
             pltpu.VMEM((16, 16, 48, 256), jnp.bfloat16),
             pltpu.VMEM((16, 384, 256), jnp.bfloat16),
-            pltpu.VMEM((16, 48, 8, 512), jnp.float32),
+            pltpu.VMEM((8, 512, 768), jnp.bfloat16),
+            pltpu.VMEM((8, 48, 16, 512), jnp.bfloat16),
+            pltpu.VMEM((8, 48, 16, 512), jnp.bfloat16),
             pltpu.SemaphoreType.DMA((N_SEM,)),
             pltpu.SemaphoreType.DMA((N_SEM,)),
             pltpu.SemaphoreType.DMA((2,)),

time: 87.4 us -> 80.8 us (0.924)
  Pallas kernels: 85 us -> 78.4 us
    pallas_call x1, Pallas kernels: 85 us -> 78.4 us  [on_device(): pl.pallas_call(kernel, out_shape=jax.ShapeDtypeStruct((512, 512), jnp.flo...]
where the time goes in v3:
time: 80.8 us; the launch traced here: 80.7 us
  Pallas kernels  78.4 us (97%)
  local copies, waits for them, and re-layouts  2.26 us (3%)
    pallas_call x1, Pallas kernels, on_device(): pl.pallas_call(kernel, out_shape=jax.ShapeDtypeStruct((512, 512), jnp.flo...  78.4 us
    unnamed x1, local copies, waits for them, and re-layouts  2.26 us

profile of v3, /device:TPU:1, one launch (start us, length us, event | category | flops | bytes accessed | tf_op | source)
XLA Modules:
  0.0 80.7 jit_solution(9911319864679477244)
XLA Ops:
  0.0 78.4 %shard_map.37 = f32[512,512]{1,0:T(8,128)} custom-call(bf16[1,3,8,8192]{3,2,1,0:T(8,128)(2,1)} %part_ref.1, s32[1,128]{1,0:T(1,128)} %epoch_ref.1, f32[1,3,128,128]{3,2,1,0:T(8,128)} %white_ref.1), custom_call_target="tpu_custom_call" | custom-call | tf_op jit(solution)/shard_map/pallas_call | solution.py:331
  78.4 2.3 %copy.5 = f32[512,512]{1,0:T(8,128)} copy(f32[512,512]{1,0:T(8,128)} %shard_map.37) | data formatting | bytes 2097152

commit v4 on v3

--- a/solution.py
+++ b/solution.py
@@ -13,23 +13,23 @@
 N_SEM = 80
 GROUPS = ((-2, 1, 5), (-3, 6, 2), (4, 1, 1))
 ORDER = (
-    "clear", ("G", "begin"), ("G", 1, True, 1), ("G", 1, True, -1), "rows", ("C", "begin"), ("mix", 0, True),
-    ("G", 2, True, 1), ("G", 2, True, -1), ("G", "yl"), "early", ("z", 1, "E0", 1), ("z", 1, "L", 1),
-    ("late", 0), ("z", 1, "L", -1), ("late", 1), ("G", 1, False, 1), ("G", 1, False, -1), ("C", 1, True, -1),
-    ("z", 1, "E0", -1), ("late", -1), ("C", 1, True, 1), ("mix", 1, True), ("G", 2, False, -1),
-    ("C", 2, True, -1), ("z", 1, "E1", -1), ("C", "yl"), ("C", 2, True, 1), ("z", 1, "E1", 1),
-    ("z", 2, "L", 1), ("late", -2), ("z", 2, "L", -1), ("late", 2), ("z", 2, "E0", 1), ("mix", 2, True),
-    ("turn", 0), ("turn", 1), ("G", 2, False, 1), ("mix", 0, False), ("z", 2, "E0", -1), ("C", 1, False, 1),
-    ("C", 1, False, -1), ("turn", -1), ("z", 2, "E1", 1), ("z", 2, "E1", -1), ("mix", 1, False),
-    ("z", 3, "L", -1), ("late", 3), ("z", 3, "L", 1), ("turn", 2), ("turn", -2), ("z", 3, "E0", -1),
-    ("late", -3), ("C", 2, False, 1), ("z", 3, "E0", 1), ("C", 2, False, -1), ("mix", 2, False),
-    ("sum", (-2, 1, 5)), ("z", 4, "L", -1), ("z", 3, "E1", -1), ("z", 4, "E0", -1), ("z", 4, "L", 1),
-    ("late", 4), ("z", 3, "E1", 1), ("turn", 3), ("z", 4, "E0", 1), ("z", 4, "E1", -1), ("turn", -3),
-    ("sum", (-3, 6, 2)), ("z", 4, "E1", 1), ("turn", 4), ("sum", (4, 1, 1)),
+    "clear", ("G", "begin"), ("G", 1, True, 1), ("G", 1, True, -1), "rows", ("C", "begin"), ("G", 2, True, 1),
+    ("G", "yl"), "early", ("z", 1, "L", 1), ("late", 0), ("z", 1, "E0", -1), ("mix", 0, True), ("late", -1),
+    ("G", 1, False, 1), ("z", 1, "L", -1), ("late", 1), ("G", 1, False, -1), ("C", 1, True, 1),
+    ("z", 1, "E0", 1), ("C", 1, True, -1), ("mix", 1, True), ("G", 2, False, 1), ("G", 2, True, -1),
+    ("C", "yl"), ("C", 2, True, -1), ("G", 2, False, -1), ("z", 1, "E1", -1), ("z", 1, "E1", 1),
+    ("z", 2, "L", -1), ("late", 2), ("z", 2, "E0", 1), ("turn", 0), ("turn", -1), ("z", 2, "L", 1),
+    ("late", -2), ("mix", 0, False), ("C", 2, True, 1), ("turn", 1), ("z", 2, "E0", -1), ("mix", 2, True),
+    ("C", 1, False, -1), ("C", 1, False, 1), ("mix", 1, False), ("z", 3, "L", -1), ("late", 3),
+    ("z", 3, "E0", 1), ("C", 2, False, 1), ("C", 2, False, -1), ("z", 2, "E1", -1), ("turn", 2),
+    ("z", 3, "E0", -1), ("z", 3, "L", 1), ("late", -3), ("z", 2, "E1", 1), ("turn", -2), ("mix", 2, False),
+    ("sum", (-2, 1, 5)), ("z", 4, "L", 1), ("z", 4, "L", -1), ("late", 4), ("z", 4, "E0", 1),
+    ("z", 3, "E1", -1), ("turn", 3), ("z", 3, "E1", 1), ("turn", -3), ("sum", (-3, 6, 2)), ("z", 4, "E1", 1),
+    ("z", 4, "E0", -1), ("z", 4, "E1", -1), ("turn", 4), ("sum", (4, 1, 1)),
 )
 
 
-def kernel(part_ref, epoch_ref, white_ref, out_ref, blocks, rows, cols, mixers, rows_t, q_high, q_low, send_sem, recv_sem, bulk_send, bulk_recv):
+def kernel(part_hbm, epoch_hbm, white_hbm, out_ref, part_ref, epoch_ref, white_ref, load_sem, blocks, rows, cols, mixers, rows_t, q_high, q_low, send_sem, recv_sem, bulk_send, bulk_recv):
     a = lax.axis_index("arc")
     p = lax.axis_index("par")
     x, yl, core = a // 4, (a // 2) % 2, a % 2
@@ -56,6 +56,13 @@
         return 0
 
     lax.fori_loop(1, 16, greet, 0)
+    loads = [
+        pltpu.make_async_copy(src, dst, load_sem.at[n])
+        for n, (src, dst) in enumerate(((part_hbm, part_ref), (epoch_hbm, epoch_ref), (white_hbm, white_ref)))
+    ]
+    for load in loads:
+        load.start()
+    loads[0].wait()
 
     for c in range(3):
         for b in range(16):
@@ -85,6 +92,9 @@
     lax.fori_loop(1, 16, send_cols, 0)
     rows[p, a] = blocks[a]
     cols[a, p] = blocks[p]
+
+    loads[1].wait()
+    loads[2].wait()
 
     row_scale = 1.0 / math.sqrt(6144)
     times = epoch_ref[...].astype(jnp.float32) / jnp.float32(511)
@@ -331,9 +341,13 @@
     return pl.pallas_call(
         kernel,
         out_shape=jax.ShapeDtypeStruct((512, 512), jnp.float32),
-        in_specs=[vmem, vmem, vmem],
+        in_specs=[pl.BlockSpec(memory_space=pl.ANY)] * 3,
         out_specs=vmem,
         scratch_shapes=[
+            pltpu.VMEM((1, 3, 8, 8192), jnp.bfloat16),
+            pltpu.VMEM((1, 128), jnp.int32),
+            pltpu.VMEM((1, 3, 128, 128), jnp.float32),
+            pltpu.SemaphoreType.DMA((3,)),
             pltpu.VMEM((16, 48, 256), jnp.bfloat16),
             pltpu.VMEM((16, 16, 48, 256), jnp.bfloat16),
             pltpu.VMEM((16, 16, 48, 256), jnp.bfloat16),

time: 80.8 us -> 78.8 us (0.975)
  Pallas kernels: 78.4 us -> 76.4 us
    pallas_call x1, Pallas kernels: 78.4 us -> 76.4 us  [on_device(): pl.pallas_call(kernel, out_shape=jax.ShapeDtypeStruct((512, 512), jnp.flo...]
where the time goes in v4:
time: 78.8 us; the launch traced here: 78.7 us
  Pallas kernels  76.4 us (97%)
  local copies, waits for them, and re-layouts  2.26 us (3%)
    pallas_call x1, Pallas kernels, on_device(): pl.pallas_call(kernel, out_shape=jax.ShapeDtypeStruct((512, 512), jnp.flo...  76.4 us
    unnamed x1, local copies, waits for them, and re-layouts  2.26 us

profile of v4, /device:TPU:1, one launch (start us, length us, event | category | flops | bytes accessed | tf_op | source)
XLA Modules:
  0.0 78.7 jit_solution(10095678728322060520)
XLA Ops:
  0.0 76.4 %shard_map.37 = f32[512,512]{1,0:T(8,128)} custom-call(bf16[1,3,8,8192]{3,2,1,0:T(8,128)(2,1)} %part_hbm.1, s32[1,128]{1,0:T(1,128)} %epoch_hbm.1, f32[1,3,128,128]{3,2,1,0:T(8,128)} %white_hbm.1), custom_call_target="tpu_custom_call" | custom-call | tf_op jit(solution)/shard_map/pallas_call | solution.py:341
  76.4 2.3 %copy.5 = f32[512,512]{1,0:T(8,128)} copy(f32[512,512]{1,0:T(8,128)} %shard_map.37) | data formatting | bytes 2097152

commit v5 on v4

--- a/solution.py
+++ b/solution.py
@@ -9,7 +9,7 @@
 
 KERNEL_GAIN = 8.0
 MESH = pl.DeviceIdType.MESH
-EARLY = 8
+EARLY = 9
 N_SEM = 80
 GROUPS = ((-2, 1, 5), (-3, 6, 2), (4, 1, 1))
 ORDER = (

time: 78.8 us -> 78.2 us (level)
  no operation moved by 1% of the time
where the time goes in v5:
time: 78.2 us; the launch traced here: 78.1 us
  Pallas kernels  75.8 us (97%)
  local copies, waits for them, and re-layouts  2.26 us (3%)
    pallas_call x1, Pallas kernels, on_device(): pl.pallas_call(kernel, out_shape=jax.ShapeDtypeStruct((512, 512), jnp.flo...  75.8 us
    unnamed x1, local copies, waits for them, and re-layouts  2.26 us

profile of v5, /device:TPU:1, one launch (start us, length us, event | category | flops | bytes accessed | tf_op | source)
XLA Modules:
  0.0 78.1 jit_solution(15907446100268817052)
XLA Ops:
  0.0 75.8 %shard_map.37 = f32[512,512]{1,0:T(8,128)} custom-call(bf16[1,3,8,8192]{3,2,1,0:T(8,128)(2,1)} %part_hbm.1, s32[1,128]{1,0:T(1,128)} %epoch_hbm.1, f32[1,3,128,128]{3,2,1,0:T(8,128)} %white_hbm.1), custom_call_target="tpu_custom_call" | custom-call | tf_op jit(solution)/shard_map/pallas_call | solution.py:341
  75.8 2.3 %copy.5 = f32[512,512]{1,0:T(8,128)} copy(f32[512,512]{1,0:T(8,128)} %shard_map.37) | data formatting | bytes 2097152

commit v6 on v5

--- a/solution.py
+++ b/solution.py
@@ -11,7 +11,7 @@
 MESH = pl.DeviceIdType.MESH
 EARLY = 9
 N_SEM = 80
-GROUPS = ((-2, 1, 5), (-3, 6, 2), (4, 1, 1))
+GROUPS = ((-1, 1, 3), (-2, 4, 2), (-3, 6, 2), (4, 1, 1))
 ORDER = (
     "clear", ("G", "begin"), ("G", 1, True, 1), ("G", 1, True, -1), "rows", ("C", "begin"), ("G", 2, True, 1),
     ("G", "yl"), "early", ("z", 1, "L", 1), ("late", 0), ("z", 1, "E0", -1), ("mix", 0, True), ("late", -1),
@@ -23,9 +23,9 @@
     ("C", 1, False, -1), ("C", 1, False, 1), ("mix", 1, False), ("z", 3, "L", -1), ("late", 3),
     ("z", 3, "E0", 1), ("C", 2, False, 1), ("C", 2, False, -1), ("z", 2, "E1", -1), ("turn", 2),
     ("z", 3, "E0", -1), ("z", 3, "L", 1), ("late", -3), ("z", 2, "E1", 1), ("turn", -2), ("mix", 2, False),
-    ("sum", (-2, 1, 5)), ("z", 4, "L", 1), ("z", 4, "L", -1), ("late", 4), ("z", 4, "E0", 1),
-    ("z", 3, "E1", -1), ("turn", 3), ("z", 3, "E1", 1), ("turn", -3), ("sum", (-3, 6, 2)), ("z", 4, "E1", 1),
-    ("z", 4, "E0", -1), ("z", 4, "E1", -1), ("turn", 4), ("sum", (4, 1, 1)),
+    ("sum", (-1, 1, 3)), ("z", 4, "L", 1), ("z", 4, "L", -1), ("late", 4), ("z", 3, "E1", -1),
+    ("z", 3, "E1", 1), ("sum", (-2, 4, 2)), ("turn", 3), ("turn", -3), ("z", 4, "E0", 1), ("z", 4, "E0", -1),
+    ("sum", (-3, 6, 2)), ("z", 4, "E1", 1), ("z", 4, "E1", -1), ("turn", 4), ("sum", (4, 1, 1)),
 )
 
 

time: 78.2 us -> 76.7 us (0.981)
  Pallas kernels: 75.8 us -> 74.3 us
    pallas_call x1, Pallas kernels: 75.8 us -> 74.3 us  [on_device(): pl.pallas_call(kernel, out_shape=jax.ShapeDtypeStruct((512, 512), jnp.flo...]
where the time goes in v6:
time: 76.7 us; the launch traced here: 76.5 us
  Pallas kernels  74.3 us (97%)
  local copies, waits for them, and re-layouts  2.26 us (3%)
    pallas_call x1, Pallas kernels, on_device(): pl.pallas_call(kernel, out_shape=jax.ShapeDtypeStruct((512, 512), jnp.flo...  74.3 us
    unnamed x1, local copies, waits for them, and re-layouts  2.26 us

profile of v6, /device:TPU:1, one launch (start us, length us, event | category | flops | bytes accessed | tf_op | source)
XLA Modules:
  0.0 76.5 jit_solution(10808065746754641168)
XLA Ops:
  0.0 74.3 %shard_map.37 = f32[512,512]{1,0:T(8,128)} custom-call(bf16[1,3,8,8192]{3,2,1,0:T(8,128)(2,1)} %part_hbm.1, s32[1,128]{1,0:T(1,128)} %epoch_hbm.1, f32[1,3,128,128]{3,2,1,0:T(8,128)} %white_hbm.1), custom_call_target="tpu_custom_call" | custom-call | tf_op jit(solution)/shard_map/pallas_call | solution.py:341
  74.3 2.3 %copy.5 = f32[512,512]{1,0:T(8,128)} copy(f32[512,512]{1,0:T(8,128)} %shard_map.37) | data formatting | bytes 2097152

commit v7 on v6

--- a/solution.py
+++ b/solution.py
@@ -88,8 +88,10 @@
         ).start()
         return 0
 
-    lax.fori_loop(1, 16, send_rows, 0)
-    lax.fori_loop(1, 16, send_cols, 0)
+    for k in range(1, 16):
+        send_rows(k, 0)
+    for k in range(1, 16):
+        send_cols(k, 0)
     rows[p, a] = blocks[a]
     cols[a, p] = blocks[p]
 

time: 76.7 us -> 76.7 us (level)
  no operation moved by 1% of the time
where the time goes in v7:
time: 76.7 us; the launch traced here: 76.6 us
  Pallas kernels  74.3 us (97%)
  local copies, waits for them, and re-layouts  2.26 us (3%)
    pallas_call x1, Pallas kernels, on_device(): pl.pallas_call(kernel, out_shape=jax.ShapeDtypeStruct((512, 512), jnp.flo...  74.3 us
    unnamed x1, local copies, waits for them, and re-layouts  2.26 us

profile of v7, /device:TPU:1, one launch (start us, length us, event | category | flops | bytes accessed | tf_op | source)
XLA Modules:
  0.0 76.6 jit_solution(5374259892533772385)
XLA Ops:
  0.0 74.3 %shard_map.37 = f32[512,512]{1,0:T(8,128)} custom-call(bf16[1,3,8,8192]{3,2,1,0:T(8,128)(2,1)} %part_hbm.1, s32[1,128]{1,0:T(1,128)} %epoch_hbm.1, f32[1,3,128,128]{3,2,1,0:T(8,128)} %white_hbm.1), custom_call_target="tpu_custom_call" | custom-call | tf_op jit(solution)/shard_map/pallas_call | solution.py:343
  74.3 2.3 %copy.5 = f32[512,512]{1,0:T(8,128)} copy(f32[512,512]{1,0:T(8,128)} %shard_map.37) | data formatting | bytes 2097152
